TPU v7x, 128 devices: a whole 4x4x4 slice. The times are simulated.
128 devices in a mesh: pair: 8 (over z_hi, y), blk: 16 (over z_lo, x, core).
Axes of the slice: x: 4, y: 4, z: 4 (z_hi: 2, z_lo: 2; z = z_hi * 2 + z_lo), core: 2. Of those that a mesh axis runs over, the one named last changes fastest.
Arguments:
- source: bfloat16 [32768, 1024], P(('pair', 'blk'))
- source_label: int32 [32768], P(('pair', 'blk')), may hold values from 0 to 7, as said below
- target: bfloat16 [32768, 1024], P(('pair', 'blk'))
- target_label: int32 [32768], P(('pair', 'blk')), may hold values from 0 to 7, as said below
Outputs:
- src_partner: float32 [32768, 1024], P(('pair', 'blk'))
- src_margin: float32 [32768], P(('pair', 'blk'))
- tgt_margin: float32 [32768], P(('pair', 'blk'))
Inputs may be any that keep to these rules, and one draw needn't show every extreme that they name: `source_label`: rows (i * 16 + k) * 256 to (i * 16 + k + 1) * 256 - 1 form block (i, k). For every k below 8, blocks (i, k) and (i, k + 8) together name every bucket exactly 64 times, so a block names one bucket at most 64 times, and in every draw some block names one bucket 64 times. `target_label`: rows (i * 16 + k) * 256 to (i * 16 + k + 1) * 256 - 1 form block (i, k). For every k below 8, blocks (i, k) and (i, k + 8) together name every bucket exactly 64 times, so a block names one bucket at most 64 times, and in every draw some block names one bucket 64 times.
All inputs are finite; a program needn't handle non-finite values.
Results may differ from a plain program's by a relative error of at most 0.0041.
Values may be sent and summed in bfloat16 or wider, within the bound.
No kernel may reach another device: no remote copies, remote signals or barrier semaphores. Data moves between devices by JAX's collectives and lax.ppermute only.
A program may use at most 128 MiB of HBM per device.

v0:
```python
import jax
import jax.numpy as jnp
from jax import lax
from jax.sharding import PartitionSpec as P

sharpness = 12.0


def normalize(row_block):
    values = row_block.astype(jnp.float32)
    square = jnp.mean(values * values, axis=-1, keepdims=True)
    return (values * lax.rsqrt(square + 1e-06)).astype(jnp.bfloat16)


def place_rows(labels, buckets, capacity):
    onehot = (labels[:, None] == jnp.arange(buckets, dtype=jnp.int32)[None, :]).astype(jnp.int32)
    before = jnp.cumsum(onehot, axis=0) - onehot
    slot_rank = jnp.sum(before * onehot, axis=1)
    return (labels * capacity + slot_rank, jnp.sum(onehot, axis=0))


def pack_rows(normed, slot_of, slot_total):
    return jnp.zeros((slot_total, normed.shape[1]), normed.dtype).at[slot_of].set(normed)


def safe_ratio(numer, denom):
    return numer / jnp.where(denom > 0.0, denom, 1.0)


def block_rows(length):
    best_size = 1
    for option in range(1, min(length, 512) + 1):
        if length % option == 0:
            best_size = option
    return best_size


def on_device(source, source_label, target, target_label):
    width = source.shape[1]
    own_rows = source.shape[0]
    buckets = lax.axis_size("pair")
    columns = lax.axis_size("blk")
    capacity = 2 * own_rows // buckets
    slot_total = buckets * capacity
    src_norm = normalize(source)
    tgt_norm = normalize(target)
    src_slot, src_count = place_rows(source_label, buckets, capacity)
    tgt_slot, tgt_count = place_rows(target_label, buckets, capacity)
    src_pack = pack_rows(src_norm, src_slot, slot_total).reshape(buckets, capacity, width)
    tgt_pack = pack_rows(tgt_norm, tgt_slot, slot_total).reshape(buckets, capacity, width)
    src_recv, tgt_recv, src_heard, tgt_heard = (
        lax.all_to_all(src_pack, "pair", split_axis=0, concat_axis=0, tiled=True),
        lax.all_to_all(tgt_pack, "pair", split_axis=0, concat_axis=0, tiled=True),
        lax.all_to_all(src_count, "pair", split_axis=0, concat_axis=0, tiled=True),
        lax.all_to_all(tgt_count, "pair", split_axis=0, concat_axis=0, tiled=True),
    )
    src_slots = src_recv.reshape(slot_total, width)
    tgt_slots = tgt_recv.reshape(slot_total, width)
    cap_spots = jnp.arange(capacity, dtype=jnp.int32)
    src_live = (cap_spots[None, :] < src_heard[:, None]).reshape(slot_total)
    tgt_live = (cap_spots[None, :] < tgt_heard[:, None]).reshape(slot_total)
    stay_live = src_live.astype(jnp.float32)
    move_live = tgt_live.astype(jnp.bfloat16)
    block_count = src_slots.shape[0]
    total_rows = columns * block_count

    def tile_weight(rows_block, live_block):
        similar = (
            lax.dot_general(
                src_slots, rows_block, (((1,), (1,)), ((), ())), preferred_element_type=jnp.float32
            )
            / width
        )
        weight = jnp.exp(sharpness * similar) * (
            stay_live[:, None] * live_block.astype(jnp.float32)[None, :]
        )
        return (similar, weight)

    zeros_rows = jnp.zeros((block_count,), jnp.float32)
    zeros_every = jnp.zeros((total_rows,), jnp.float32)
    held_init = jnp.zeros((1, 1), jnp.float32)
    first_init = (
        jnp.zeros((block_count, width), jnp.float32),
        zeros_rows,
        zeros_rows,
        zeros_every,
        zeros_every,
        held_init,
    )
    first_row = jnp.int32(0)
    part_rows = lax.all_gather(tgt_slots, "blk", axis=0, tiled=True)
    part_live = lax.all_gather(move_live, "blk", axis=0, tiled=True)
    length = part_rows.shape[0]
    step_rows = block_rows(length)

    def first_inner_step(block_index, state):
        partner_acc, fwd_total, fwd_sum, bwd_total, bwd_sum, held_tiles = state
        offset = block_index * step_rows
        rows_block = lax.dynamic_slice_in_dim(part_rows, offset, step_rows, 0)
        live_block = lax.dynamic_slice_in_dim(part_live, offset, step_rows, 0)
        similar, weight = tile_weight(rows_block, live_block)
        weighted = weight * similar
        partner_acc = partner_acc + jnp.dot(
            weight.astype(jnp.bfloat16), rows_block, preferred_element_type=jnp.float32
        )
        fwd_total = fwd_total + jnp.sum(weight, axis=1)
        fwd_sum = fwd_sum + jnp.sum(weighted, axis=1)
        bwd_total = lax.dynamic_update_slice_in_dim(
            bwd_total, jnp.sum(weight, axis=0), first_row + offset, 0
        )
        bwd_sum = lax.dynamic_update_slice_in_dim(
            bwd_sum, jnp.sum(weighted, axis=0), first_row + offset, 0
        )
        return (partner_acc, fwd_total, fwd_sum, bwd_total, bwd_sum, held_tiles)

    partner_acc, fwd_total, fwd_sum, part_total, part_sum, held_tiles = lax.fori_loop(
        0, length // step_rows, first_inner_step, first_init
    )
    summed_total, summed_weighted = lax.psum((part_total, part_sum), "blk")
    bwd_every = safe_ratio(summed_weighted, summed_total)
    own_index = lax.axis_index("blk")
    own_total = lax.dynamic_slice_in_dim(summed_total, own_index * block_count, block_count, 0)
    own_bwd = lax.dynamic_slice_in_dim(bwd_every, own_index * block_count, block_count, 0)
    fwd_stat = safe_ratio(fwd_sum, fwd_total)
    second_first_row = jnp.int32(0)
    second_part_rows = lax.all_gather(tgt_slots, "blk", axis=0, tiled=True)
    second_part_live = lax.all_gather(move_live, "blk", axis=0, tiled=True)
    length = second_part_rows.shape[0]
    second_step_rows = block_rows(length)

    def second_inner_step(block_index, state):
        back_acc, fore_part = state
        offset = block_index * second_step_rows
        rows_block = lax.dynamic_slice_in_dim(second_part_rows, offset, second_step_rows, 0)
        live_block = lax.dynamic_slice_in_dim(second_part_live, offset, second_step_rows, 0)
        similar, weight = tile_weight(rows_block, live_block)
        bwd_block = lax.dynamic_slice_in_dim(
            bwd_every, second_first_row + offset, second_step_rows, 0
        )
        back_acc = back_acc + jnp.dot(weight, bwd_block, precision=lax.Precision.HIGHEST)
        fore_block = jnp.dot(fwd_stat, weight, precision=lax.Precision.HIGHEST)
        fore_part = lax.dynamic_update_slice_in_dim(
            fore_part, fore_block, second_first_row + offset, 0
        )
        return (back_acc, fore_part)

    back_acc, fore_part = lax.fori_loop(
        0, length // second_step_rows, second_inner_step, (zeros_rows, zeros_every)
    )
    fore_own = lax.psum_scatter(
        fore_part.reshape(columns, block_count), "blk", scatter_dimension=0, tiled=True
    )[0]
    partner = safe_ratio(partner_acc, fwd_total[:, None])
    src_margin = fwd_stat - 0.5 * (fwd_stat + safe_ratio(back_acc, fwd_total))
    tgt_margin = own_bwd - 0.5 * (own_bwd + safe_ratio(fore_own, own_total))
    back_partner, back_src, back_tgt = (
        lax.all_to_all(
            partner.reshape(buckets, capacity, width),
            "pair",
            split_axis=0,
            concat_axis=0,
            tiled=True,
        ),
        lax.all_to_all(
            src_margin.reshape(buckets, capacity), "pair", split_axis=0, concat_axis=0, tiled=True
        ),
        lax.all_to_all(
            tgt_margin.reshape(buckets, capacity), "pair", split_axis=0, concat_axis=0, tiled=True
        ),
    )
    partner_out = back_partner.reshape(slot_total, width)[src_slot]
    src_out = back_src.reshape(slot_total)[src_slot]
    tgt_out = back_tgt.reshape(slot_total)[tgt_slot]
    return (partner_out, src_out, tgt_out)


def solution(mesh):
    return jax.shard_map(
        on_device,
        mesh=mesh,
        in_specs=(
            P(("pair", "blk"), None),
            P(("pair", "blk")),
            P(("pair", "blk"), None),
            P(("pair", "blk")),
        ),
        out_specs=(P(("pair", "blk"), None), P(("pair", "blk")), P(("pair", "blk"))),
        check_vma=False,
    )
```

profile of v0, /device:TPU:6, one launch (start us, length us, event | category | flops | bytes accessed | tf_op | source)
XLA Modules:
  0.0 529.9 jit_solution(6003493025504286049)
XLA Ops:
  14.1 24.9 %all_to_all.51 = bf16[8,64,1024]{2,1,0:T(8,128)(2,1)} all-to-all(bf16[8,64,1024]{2,1,0:T(8,128)(2,1)S(1)} %bitcast.88), channel_id=1, replica_groups=mesh['pair'=8,'blk'=16] {'pair'}, dimensions={0} | all-to-all | bytes 2097152 | tf_op jit(solution)/shard_map/all_to_all | solution.py:53
  39.6 3.3 all-to-all-start.3
  44.2 2.7 scatter_custom_fusion.1
  46.9 3.6 all-to-all-done.3
  50.5 11.0 %all_to_all.52 = s32[8,1,1]{2,1,0:T(1,128)S(1)} all-to-all(s32[8,1,1]{2,1,0:T(1,128)S(1)} %copy.10), channel_id=1, replica_groups=mesh['pair'=8,'blk'=16] {'pair'}, dimensions={0} | all-to-all | bytes 64 | tf_op jit(solution)/shard_map/all_to_all | solution.py:54
  61.5 4.2 all-to-all-start.1
  66.9 15.6 %all-gather = bf16[16,1,512]{2,1,0:T(2,128)(2,1)S(1)} all-gather(bf16[1,1,512]{2,1,0:T(2,128)(2,1)S(1)} %reshape.176), channel_id=1, replica_groups=mesh['pair'=8,'blk'=16] {'blk'}, dimensions={0}, use_global_device_ids=true | all-gather | bytes 17408 | tf_op jit(solution)/shard_map/all_gather | solution.py:92
  82.8 56.6 %all-gather.3.cloned.1.call-done = bf16[8192,1024]{1,0:T(8,128)(2,1)} async-done(((bf16[512,1024]{1,0:T(8,128)(2,1)}), bf16[8192,1024]{1,0:T(8,128)(2,1)}) %all-gather.3.cloned.1.call-update) | async-done | bytes 16777232 | tf_op jit(solution)/shard_map/all_gather | solution.py:91
  139.4 91.3 %while.42 = (s32[]{:T(128)}, f32[512,1024]{1,0:T(8,128)S(1)}, f32[512]{0:T(512)S(1)}, f32[512]{0:T(512)S(1)}, f32[8192]{0:T(1024)S(1)}, /*index=5*/f32[8192]{0:T...) while((s32[]{:T(128)}, f32[512,1024]{1,0:T(8,128)S(1)}, ...), condition=%wide.region_17.18_spmd.clone, body=%wide.region_12.17_spmd.clone.sunk | while | flops 1078199808 | bytes 9483506 | solution.py:116
  139.6 2.6 fusion.76
  145.3 2.6 fusion.76
  151.1 2.6 fusion.76
  156.8 2.6 fusion.76
  162.5 2.6 fusion.76
  168.2 2.6 fusion.76
  173.9 2.6 fusion.76
  179.7 2.6 fusion.76
  185.4 2.6 fusion.76
  191.1 2.6 fusion.76
  196.8 2.6 fusion.76
  202.5 2.6 fusion.76
  208.2 2.6 fusion.76
  214.0 2.6 fusion.76
  231.4 104.7 %all-reduce.4.cloned.1.call-done = (f32[8192]{0:T(1024)}, f32[8192]{0:T(1024)}) async-done(((f32[8192]{0:T(1024)}, f32[8192]{0:T(1024)}), (f32[8192]{0:T(1024)}, f32[8192]{0:T(1024)})) %all-reduce.4.cloned.1.call-update) | async-done | bytes 65552 | tf_op jit(solution)/shard_map/psum | solution.py:119
  336.9 71.7 %while.43 = (s32[]{:T(128)}, f32[512]{0:T(512)S(1)}, f32[8192]{0:T(1024)S(1)}, bf16[8192,1024]{1,0:T(8,128)(2,1)}, bf16[512,1024]{1,0:T(8,128)(2,1)}, /*index=5*...) while((s32[]{:T(128)}, f32[512]{0:T(512)S(1)}, ...), condition=%wide.region_21.22_spmd.clone, body=%wide.region_20.21_spmd.clone.sunk | while | flops 543951360 | bytes 5278949 | solution.py:147
  408.6 52.9 %all-reduce = f32[16,512]{1,0:T(8,128)S(1)} all-reduce(f32[16,512]{1,0:T(8,128)S(1)} %reshape.127), channel_id=2, replica_groups=mesh['pair'=8,'blk'=16] {'blk'}, use_global_device_ids=true, to_apply=%region_22.23.clone | all-reduce | flops 8192 | bytes 65536
  463.6 6.9 %all-to-all-start.6 = ((f32[8,1,64]{2,1,0:T(1,128)}), f32[8,1,64]{2,1,0:T(1,128)S(1)}, u32[]{:S(2)}, u32[]{:S(2)}) async-start(f32[8,1,64]{2,1,0:T(1,128)} %all_to_all.42), calls=%async_computation.6 | async-start | bytes 8192 | tf_op jit(solution)/shard_map/all_to_all | solution.py:167
  471.2 7.0 %all-to-all-done.6 = f32[8,1,64]{2,1,0:T(1,128)S(1)} async-done(((f32[8,1,64]{2,1,0:T(1,128)}), f32[8,1,64]{2,1,0:T(1,128)S(1)}, u32[]{:S(2)}, u32[]{:S(2)}) %all-to-all-start.6) | async-done | bytes 2080 | tf_op jit(solution)/shard_map/all_to_all | solution.py:167
  478.2 3.3 all-to-all-start.5
  483.1 5.9 %all-to-all-done.5 = f32[8,1,64]{2,1,0:T(1,128)S(1)} async-done(((f32[8,1,64]{2,1,0:T(1,128)}), f32[8,1,64]{2,1,0:T(1,128)S(1)}, u32[]{:S(2)}, u32[]{:S(2)}) %all-to-all-start.5) | async-done | bytes 2080 | tf_op jit(solution)/shard_map/all_to_all | solution.py:164
  489.0 3.6 all-to-all-start.4
  499.6 21.4 %all-to-all-done.4 = f32[8,64,1024]{2,1,0:T(8,128)S(1)} async-done(((f32[8,64,1024]{2,1,0:T(8,128)}), f32[8,64,1024]{2,1,0:T(8,128)S(1)}, u32[]{:S(2)}, u32[]{:S(2)}) %all-to-all-start.4) | async-done | bytes 2097184 | tf_op jit(solution)/shard_map/all_to_all | solution.py:157
  (327 shorter events, 150.3 us)
Async XLA Ops:
  7.2 132.2 %all-gather.3.cloned.1.call-start = ((), (), s32[]{:S(2)}) async-start(), calls=%async_computation.7 | async-start | bytes 17825792 | tf_op jit(solution)/shard_map/all_gather | solution.py:91
  11.5 31.4 %copy-start.3 = (s32[256]{0:T(256)S(1)}, s32[256]{0:T(256)}, u32[]{:S(2)}) copy-start(s32[256]{0:T(256)} %param.9) | copy-start | bytes 3076
  11.5 32.5 %copy-start = (bf16[256,1024]{1,0:T(8,128)(2,1)S(1)}, bf16[256,1024]{1,0:T(8,128)(2,1)}, u32[]{:S(2)}) copy-start(bf16[256,1024]{1,0:T(8,128)(2,1)} %param.8) | copy-start | bytes 1572868
  39.6 10.8 %all-to-all-start.3 = ((s32[8,1,1]{2,1,0:T(1,128)}), s32[8,1,1]{2,1,0:T(1,128)S(1)}, u32[]{:S(2)}, u32[]{:S(2)}) async-start(s32[8,1,1]{2,1,0:T(1,128)} %copy.9), calls=%async_computation.3 | async-start | bytes 8192 | tf_op jit(solution)/shard_map/all_to_all | solution.py:55
  44.0 21.8 %copy-start.4 = (u32[128]{0:T(128)S(1)}, u32[128]{0:T(128)}, u32[]{:S(2)}) copy-start(u32[128]{0:T(128)} %constant.168) | copy-start | bytes 1540
  61.5 21.3 %all-to-all-start.1 = ((bf16[8,64,1024]{2,1,0:T(8,128)(2,1)}), bf16[8,64,1024]{2,1,0:T(8,128)(2,1)}, u32[]{:S(2)}, u32[]{:S(2)}) async-start(bf16[8,64,1024]{2,1,0:T(8,128)(2,1)} %bitcast.8), calls=%async_computation.1 | async-start | bytes 2097152 | tf_op jit(solution)/shard_map/all_to_all | solution.py:52
  65.7 270.3 %all-reduce.4.cloned.1.call-start = ((), (), s32[]{:S(2)}) async-start(), calls=%async_computation.8 | async-start | bytes 131072 | tf_op jit(solution)/shard_map/psum | solution.py:119
  230.7 0.6 copy-start.1
  230.7 0.6 copy-start.2
  463.6 14.5 %all-to-all-start.6 = ((f32[8,1,64]{2,1,0:T(1,128)}), f32[8,1,64]{2,1,0:T(1,128)S(1)}, u32[]{:S(2)}, u32[]{:S(2)}) async-start(f32[8,1,64]{2,1,0:T(1,128)} %all_to_all.42), calls=%async_computation.6 | async-start | bytes 8192 | tf_op jit(solution)/shard_map/all_to_all | solution.py:167
  478.2 10.8 %all-to-all-start.5 = ((f32[8,1,64]{2,1,0:T(1,128)}), f32[8,1,64]{2,1,0:T(1,128)S(1)}, u32[]{:S(2)}, u32[]{:S(2)}) async-start(f32[8,1,64]{2,1,0:T(1,128)} %all_to_all.40), calls=%async_computation.5 | async-start | bytes 8192 | tf_op jit(solution)/shard_map/all_to_all | solution.py:164
  489.0 32.1 %all-to-all-start.4 = ((f32[8,64,1024]{2,1,0:T(8,128)}), f32[8,64,1024]{2,1,0:T(8,128)S(1)}, u32[]{:S(2)}, u32[]{:S(2)}) async-start(f32[8,64,1024]{2,1,0:T(8,128)} %bitcast.86), calls=%async_computation.4 | async-start | bytes 4194304 | tf_op jit(solution)/shard_map/all_to_all | solution.py:157
Sparse Core Ops, SparseCore 0:
  39.1 100.2 all-gather.2
  231.5 104.5 all-reduce.3
where the time goes:
time: 532 us; the launch traced here: 530 us
  waiting for transfers between devices  199 us (37%)
  matrix products  142 us (27%)
  blocking collectives  104 us (20%)
  local copies, waits for them, and re-layouts  27.3 us (5%)
  starting transfers between devices  21.4 us (4%)
  other arithmetic  20.6 us (4%)
  between operations  14.3 us (3%)
    psum x1, waiting for transfers between devices, on_device(): summed_total, summed_weighted = lax.psum((part_total, part_sum), 'blk')  105 us
    dot_general x32, matrix products, tile_weight(): lax.dot_general(src_slots, rows_block, (((1,), (1,)), ((), ())), preferre...  79 us
    all_gather x1, waiting for transfers between devices, on_device(): part_rows = lax.all_gather(tgt_slots, 'blk', axis=0, tiled=True)  56.6 us
    unnamed x1, blocking collectives  52.9 us
    dot_general x16, matrix products, first_inner_step(): jnp.dot(weight.astype(jnp.bfloat16), rows_block, preferred_element_type=j...  36.7 us
    all_to_all x1, blocking collectives, on_device(): lax.all_to_all(tgt_pack, 'pair', split_axis=0, concat_axis=0, tiled=True)  24.9 us
    all_to_all x1, waiting for transfers between devices, on_device(): lax.all_to_all(partner.reshape(buckets, capacity, width), 'pair', split_a...  21.4 us
    dot_general x16, matrix products, second_inner_step(): fore_block = jnp.dot(fwd_stat, weight, precision=lax.Precision.HIGHEST)  15.7 us
  transfers between devices with their start and end apart: 7, of which 6 were waited for; matrix products, arithmetic and copies ran while one was open for 3% of the time, Pallas kernels for 0%

commit v1 on v0

--- a/solution.py
+++ b/solution.py
@@ -88,7 +88,9 @@
         held_init,
     )
     first_row = jnp.int32(0)
-    part_rows = lax.all_gather(tgt_slots, "blk", axis=0, tiled=True)
+    part_rows = jnp.concatenate(
+        lax.all_to_all(jnp.stack([tgt_slots] * lax.axis_size("blk")), "blk", 0, 0), axis=0
+    )
     part_live = lax.all_gather(move_live, "blk", axis=0, tiled=True)
     length = part_rows.shape[0]
     step_rows = block_rows(length)

time: 532 us -> 810 us (1.52)
  blocking collectives: 104 us -> 318 us
  waiting for transfers between devices: 199 us -> 246 us
  starting transfers between devices: 21.4 us -> 30.3 us
    all_gather x1, blocking collectives: 15.6 us -> 233 us  [on_device(): part_live = lax.all_gather(move_live, 'blk', axis=0, tiled=True)]
    all_gather x1, waiting for transfers between devices: 56.6 us -> 96.6 us  [on_device(): second_part_rows = lax.all_gather(tgt_slots, 'blk', axis=0, tiled=True)]
    all_to_all x1 -> x2, waiting for transfers between devices: 0.01 us -> 13.2 us  [the longest x1 13.2 us: on_device(): lax.all_to_all(tgt_pack, 'pair', split_axis=0, concat_axis=0, tiled=True)]
  transfers between devices with their start and end apart: 7 -> 8, of which waited for: 6 -> 6; matrix products, arithmetic and copies ran while one was open for 3% -> 3% of each run, Pallas kernels for 0% -> 0%
where the time goes in v1:
time: 810 us; the launch traced here: 808 us
  blocking collectives  318 us (39%)
  waiting for transfers between devices  246 us (30%)
  matrix products  143 us (18%)
  local copies, waits for them, and re-layouts  33.3 us (4%)
  starting transfers between devices  30.3 us (4%)
  other arithmetic  22 us (3%)
  between operations  14.3 us (2%)
    all_gather x1, blocking collectives, on_device(): part_live = lax.all_gather(move_live, 'blk', axis=0, tiled=True)  233 us
    psum x1, waiting for transfers between devices, on_device(): summed_total, summed_weighted = lax.psum((part_total, part_sum), 'blk')  101 us
    all_gather x1, waiting for transfers between devices, on_device(): second_part_rows = lax.all_gather(tgt_slots, 'blk', axis=0, tiled=True)  96.6 us
    dot_general x32, matrix products, tile_weight(): lax.dot_general(src_slots, rows_block, (((1,), (1,)), ((), ())), preferre...  79.2 us
    unnamed x1, blocking collectives  50.3 us
    dot_general x16, matrix products, first_inner_step(): jnp.dot(weight.astype(jnp.bfloat16), rows_block, preferred_element_type=j...  37.2 us
    all_to_all x1, waiting for transfers between devices, on_device(): lax.all_to_all(partner.reshape(buckets, capacity, width), 'pair', split_a...  21.4 us
    all_to_all x1, blocking collectives, on_device(): lax.all_to_all(src_pack, 'pair', split_axis=0, concat_axis=0, tiled=True)  20.4 us
  transfers between devices with their start and end apart: 8, of which 6 were waited for; matrix products, arithmetic and copies ran while one was open for 3% of the time, Pallas kernels for 0%

profile of v1, /device:TPU:6, one launch (start us, length us, event | category | flops | bytes accessed | tf_op | source)
XLA Modules:
  0.0 807.7 jit_solution(14959612080226981171)
XLA Ops:
  10.2 7.8 all-to-all-start.4
  22.5 3.2 scatter_custom_fusion
  25.7 14.7 %all_to_all.56 = s32[8,1,1]{2,1,0:T(1,128)S(1)} all-to-all(s32[8,1,1]{2,1,0:T(1,128)S(1)} %copy.10), channel_id=1, replica_groups=mesh['pair'=8,'blk'=16] {'pair'}, dimensions={0} | all-to-all | bytes 64 | tf_op jit(solution)/shard_map/all_to_all | solution.py:54
  40.3 3.6 all-to-all-start
  46.1 13.2 %all-to-all-done = bf16[8,64,1024]{2,1,0:T(8,128)(2,1)S(1)} async-done(((bf16[8,64,1024]{2,1,0:T(8,128)(2,1)}), bf16[8,64,1024]{2,1,0:T(8,128)(2,1)S(1)}, u32[]{:S(2)}, u32[]{:S(2)}) %all-to-all-start) | async-done | bytes 1048608 | tf_op jit(solution)/shard_map/all_to_all | solution.py:53
  59.3 20.4 %all_to_all.57 = bf16[8,64,1024]{2,1,0:T(8,128)(2,1)} all-to-all(bf16[8,64,1024]{2,1,0:T(8,128)(2,1)S(1)} %bitcast.90), channel_id=1, replica_groups=mesh['pair'=8,'blk'=16] {'pair'}, dimensions={0} | all-to-all | bytes 2097152 | tf_op jit(solution)/shard_map/all_to_all | solution.py:52
  79.8 5.9 stack.3
  85.7 5.4 all-to-all-start.1
  91.6 232.9 %all-gather = bf16[16,1,512]{2,1,0:T(2,128)(2,1)S(1)} all-gather(bf16[1,1,512]{2,1,0:T(2,128)(2,1)S(1)} %reshape.179), channel_id=1, replica_groups=mesh['pair'=8,'blk'=16] {'blk'}, dimensions={0}, use_global_device_ids=true | all-gather | bytes 17408 | tf_op jit(solution)/shard_map/all_gather | solution.py:94
  324.8 92.0 %while.42 = (s32[]{:T(128)}, f32[512,1024]{1,0:T(8,128)S(1)}, f32[512]{0:T(512)S(1)}, f32[512]{0:T(512)S(1)}, f32[8192]{0:T(1024)S(1)}, /*index=5*/f32[8192]{0:T...) while((s32[]{:T(128)}, f32[512,1024]{1,0:T(8,128)S(1)}, ...), condition=%wide.region_17.18_spmd.clone, body=%wide.region_12.17_spmd.clone.sunk | while | flops 1078199808 | bytes 9483506 | solution.py:118
  325.1 2.6 fusion.76
  330.8 2.6 fusion.76
  336.6 2.6 fusion.76
  342.4 2.6 fusion.76
  348.1 2.6 fusion.76
  353.9 2.6 fusion.76
  359.6 2.6 fusion.76
  365.4 2.6 fusion.76
  371.2 2.6 fusion.76
  376.9 2.6 fusion.76
  382.7 2.6 fusion.76
  388.4 2.6 fusion.76
  418.9 101.3 %all-reduce.4.cloned.1.call-done = (f32[8192]{0:T(1024)}, f32[8192]{0:T(1024)}) async-done(((f32[8192]{0:T(1024)}, f32[8192]{0:T(1024)}), (f32[8192]{0:T(1024)}, f32[8192]{0:T(1024)})) %all-reduce.4.cloned.1.call-update) | async-done | bytes 65552 | tf_op jit(solution)/shard_map/psum | solution.py:121
  520.9 96.6 %all-gather.3.cloned.1.call-done = bf16[8192,1024]{1,0:T(8,128)(2,1)} async-done(((bf16[512,1024]{1,0:T(8,128)(2,1)}), bf16[8192,1024]{1,0:T(8,128)(2,1)}) %all-gather.3.cloned.1.call-update) | async-done | bytes 16777232 | tf_op jit(solution)/shard_map/all_gather | solution.py:128
  617.5 71.7 %while.43 = (s32[]{:T(128)}, f32[512]{0:T(512)S(1)}, f32[8192]{0:T(1024)S(1)}, bf16[8192,1024]{1,0:T(8,128)(2,1)}, bf16[512,1024]{1,0:T(8,128)(2,1)}, /*index=5*...) while((s32[]{:T(128)}, f32[512]{0:T(512)S(1)}, ...), condition=%wide.region_21.22_spmd.clone, body=%wide.region_20.21_spmd.clone.sunk | while | flops 543951360 | bytes 5278949 | solution.py:149
  689.3 50.3 %all-reduce = f32[16,512]{1,0:T(8,128)S(1)} all-reduce(f32[16,512]{1,0:T(8,128)S(1)} %reshape.130), channel_id=2, replica_groups=mesh['pair'=8,'blk'=16] {'blk'}, use_global_device_ids=true, to_apply=%region_22.23.clone | all-reduce | flops 8192 | bytes 65536
  741.7 6.6 all-to-all-start.7
  749.0 7.0 all-to-all-done.7
  755.9 3.3 all-to-all-start.6
  760.8 5.9 all-to-all-done.6
  766.8 3.6 all-to-all-start.5
  777.4 21.4 %all-to-all-done.5 = f32[8,64,1024]{2,1,0:T(8,128)S(1)} async-done(((f32[8,64,1024]{2,1,0:T(8,128)}), f32[8,64,1024]{2,1,0:T(8,128)S(1)}, u32[]{:S(2)}, u32[]{:S(2)}) %all-to-all-start.5) | async-done | bytes 2097184 | tf_op jit(solution)/shard_map/all_to_all | solution.py:159
  (332 shorter events, 157.8 us)
Async XLA Ops:
  10.2 15.5 %all-to-all-start.4 = ((s32[8,1,1]{2,1,0:T(1,128)}), s32[8,1,1]{2,1,0:T(1,128)S(1)}, u32[]{:S(2)}, u32[]{:S(2)}) async-start(s32[8,1,1]{2,1,0:T(1,128)} %copy.9), calls=%async_computation.4 | async-start | bytes 8192 | tf_op jit(solution)/shard_map/all_to_all | solution.py:55
  18.7 25.2 %copy-start.1 = (bf16[256,1024]{1,0:T(8,128)(2,1)S(1)}, bf16[256,1024]{1,0:T(8,128)(2,1)}, u32[]{:S(2)}) copy-start(bf16[256,1024]{1,0:T(8,128)(2,1)} %param.8) | copy-start | bytes 1572868
  22.5 21.6 %copy-start.4 = (s32[256]{0:T(256)S(1)}, s32[256]{0:T(256)}, u32[]{:S(2)}) copy-start(s32[256]{0:T(256)} %param.9) | copy-start | bytes 3076
  40.3 19.0 %all-to-all-start = ((bf16[8,64,1024]{2,1,0:T(8,128)(2,1)}), bf16[8,64,1024]{2,1,0:T(8,128)(2,1)S(1)}, u32[]{:S(2)}, u32[]{:S(2)}) async-start(bf16[8,64,1024]{2,1,0:T(8,128)(2,1)} %bitcast.3), calls=%async_computation | async-start | bytes 2097152 | tf_op jit(solution)/shard_map/all_to_all | solution.py:53
  59.3 26.4 %copy-start = (bf16[8,64,1024]{2,1,0:T(8,128)(2,1)}, bf16[8,64,1024]{2,1,0:T(8,128)(2,1)S(1)}, u32[]{:S(2)}) copy-start(bf16[8,64,1024]{2,1,0:T(8,128)(2,1)S(1)} %all-to-all-done) | copy-start | bytes 3145732
  85.7 239.1 %all-to-all-start.1 = ((bf16[16,512,1024]{2,1,0:T(8,128)(2,1)}), bf16[16,512,1024]{2,1,0:T(8,128)(2,1)}, u32[]{:S(2)}, u32[]{:S(2)}) async-start(bf16[16,512,1024]{2,1,0:T(8,128)(2,1)} %stack.3), calls=%async_computation.1 | async-start | bytes 33554432 | tf_op jit(solution)/shard_map/all_to_all | solution.py:92
  91.1 429.0 %all-reduce.4.cloned.1.call-start = ((), (), s32[]{:S(2)}) async-start(), calls=%async_computation.9 | async-start | bytes 131072 | tf_op jit(solution)/shard_map/psum | solution.py:121
  324.8 93.5 %copy-start.5 = (u32[128]{0:T(128)S(1)}, u32[128]{0:T(128)}, u32[]{:S(2)}) copy-start(u32[128]{0:T(128)} %constant.168) | copy-start | bytes 1540
  416.9 0.6 copy-start.2
  416.9 0.6 copy-start.3
  417.5 200.0 %all-gather.3.cloned.1.call-start = ((), (), s32[]{:S(2)}) async-start(), calls=%async_computation.8 | async-start | bytes 17825792 | tf_op jit(solution)/shard_map/all_gather | solution.py:128
  741.7 14.3 %all-to-all-start.7 = ((f32[8,1,64]{2,1,0:T(1,128)}), f32[8,1,64]{2,1,0:T(1,128)S(1)}, u32[]{:S(2)}, u32[]{:S(2)}) async-start(f32[8,1,64]{2,1,0:T(1,128)} %all_to_all.46), calls=%async_computation.7 | async-start | bytes 8192 | tf_op jit(solution)/shard_map/all_to_all | solution.py:169
  755.9 10.8 %all-to-all-start.6 = ((f32[8,1,64]{2,1,0:T(1,128)}), f32[8,1,64]{2,1,0:T(1,128)S(1)}, u32[]{:S(2)}, u32[]{:S(2)}) async-start(f32[8,1,64]{2,1,0:T(1,128)} %all_to_all.44), calls=%async_computation.6 | async-start | bytes 8192 | tf_op jit(solution)/shard_map/all_to_all | solution.py:166
  766.8 32.1 %all-to-all-start.5 = ((f32[8,64,1024]{2,1,0:T(8,128)}), f32[8,64,1024]{2,1,0:T(8,128)S(1)}, u32[]{:S(2)}, u32[]{:S(2)}) async-start(f32[8,64,1024]{2,1,0:T(8,128)} %bitcast.89), calls=%async_computation.5 | async-start | bytes 4194304 | tf_op jit(solution)/shard_map/all_to_all | solution.py:159
Sparse Core Ops, SparseCore 0:
  417.6 102.4 all-reduce.3
  522.5 94.9 all-gather.2
